TPU v7x, 32 devices: a whole 2x2x4 slice. The times are simulated.
32 devices in a mesh: rep: 4 (over z), grp: 8 (over y, x, core).
Axes of the slice: x: 2, y: 2, z: 4, core: 2. Of those that a mesh axis runs over, the one named last changes fastest.
Arguments:
- tokens: bfloat16 [192, 197, 768], P(('rep', 'grp')), may hold values from -6 to 6
- cotangent: bfloat16 [192, 197, 768], P(('rep', 'grp')), may hold values from -6 to 6
- heads_in: bfloat16 [768, 2304], P('grp'), may hold values from -0.3125 to 0.3125
- heads_out: bfloat16 [768, 768], P('grp'), may hold values from -0.875 to 0.875
- slot_router: bfloat16 [768, 4], P('grp'), may hold values from -0.109375 to 0.109375
- first_gain: bfloat16 [768], P('grp'), may hold values from 0.5 to 1.5
- second_gain: bfloat16 [768], P('grp'), may hold values from 0.5 to 1.5
- expert_in: bfloat16 [8, 768, 1536], P('grp'), may hold values from -3 to 3
- expert_out: bfloat16 [8, 1536, 768], P('grp'), may hold values from -0.21875 to 0.21875
Outputs:
- output: bfloat16 [192, 197, 768], P(('rep', 'grp'))
- token_grad: bfloat16 [192, 197, 768], P(('rep', 'grp'))
- heads_in_grad: float32 [768, 2304], P('grp')
- heads_out_grad: float32 [768, 768], P('grp')
- router_grad: float32 [768, 4], P('grp')
- first_gain_grad: float32 [768], P('grp')
- second_gain_grad: float32 [768], P('grp')
- expert_in_grad: float32 [8, 768, 1536], P('grp')
- expert_out_grad: float32 [8, 1536, 768], P('grp')
All inputs are finite; a program needn't handle non-finite values.
Results may differ from a plain program's by a relative error of at most 0.019.
Values may be sent and summed in bfloat16 or wider, within the bound.
No kernel may reach another device: no remote copies, remote signals or barrier semaphores. Data moves between devices by JAX's collectives and lax.ppermute only.
A program may use at most 192 MiB of HBM per device.

v0:
```python
import jax
import jax.numpy as jnp
from jax import lax
from jax.sharding import PartitionSpec as P

HEADS = 12


def mult(form, left, right):
    return jnp.einsum(form, left, right, preferred_element_type=jnp.float32)


def layer_stats(values):
    center = values - jnp.mean(values, axis=-1, keepdims=True)
    spread = jnp.mean(center * center, axis=-1, keepdims=True)
    factor = lax.rsqrt(spread + 1e-06)
    return (center * factor, factor)


def norm_back(grad_norm, gain, normed, factor):
    scaled = grad_norm * gain
    inner = (
        scaled
        - jnp.mean(scaled, axis=-1, keepdims=True)
        - normed * jnp.mean(scaled * normed, axis=-1, keepdims=True)
    )
    return (factor * inner, jnp.sum(grad_norm * normed, axis=(0, 1)))


def activate(values):
    return jax.nn.gelu(values, approximate=True)


def per_device(
    tokens,
    cotangent,
    heads_in,
    heads_out,
    slot_router,
    first_gain,
    second_gain,
    expert_in,
    expert_out,
):
    images, places, features = tokens.shape
    head_count = HEADS
    head_size = features // head_count
    scaling = head_size ** (-0.5)
    gathered = (
        lax.all_gather(heads_in, "grp", axis=0, tiled=True),
        lax.all_gather(heads_out, "grp", axis=0, tiled=True),
        lax.all_gather(slot_router, "grp", axis=0, tiled=True),
        lax.all_gather(first_gain, "grp", axis=0, tiled=True),
        lax.all_gather(second_gain, "grp", axis=0, tiled=True),
    )
    full_in, full_out, full_router, gain_a, gain_b = gathered
    gain_one = gain_a.astype(jnp.float32)
    gain_two = gain_b.astype(jnp.float32)
    source = tokens.astype(jnp.float32)
    normed_one, factor_one = layer_stats(source)
    act_one = (normed_one * gain_one).astype(jnp.bfloat16)
    joint = mult("bnd,df->bnf", act_one, full_in).astype(jnp.bfloat16)
    split = joint.reshape(images, places, 3, head_count, head_size)
    query, keys, values = (split[:, :, 0], split[:, :, 1], split[:, :, 2])
    scores = mult("bqhe,bkhe->bhqk", query, keys) * scaling
    maximum = jnp.max(scores, axis=-1, keepdims=True)
    logsum = maximum + jnp.log(jnp.sum(jnp.exp(scores - maximum), axis=-1, keepdims=True))
    probs = jnp.exp(scores - logsum).astype(jnp.bfloat16)
    mixed = (
        mult("bhqk,bkhe->bqhe", probs, values)
        .reshape(images, places, features)
        .astype(jnp.bfloat16)
    )
    resid = source + mult("bnd,de->bne", mixed, full_out)
    normed_two, factor_two = layer_stats(resid)
    act_two = (normed_two * gain_two).astype(jnp.bfloat16)
    logits = mult("bnd,de->bne", act_two, full_router)
    dispatch = jax.nn.softmax(logits, axis=1)
    combine = jax.nn.softmax(logits, axis=2)
    disp_low = dispatch.astype(jnp.bfloat16)
    comb_low = combine.astype(jnp.bfloat16)
    slots = mult("bne,bnd->bed", disp_low, act_two).astype(jnp.bfloat16)
    received = lax.all_to_all(
        jnp.repeat(slots, 2, axis=1), "grp", split_axis=1, concat_axis=0, tiled=True
    )
    rows = received.reshape(-1, features)
    piece_in = expert_in[0]
    piece_out = expert_out[0]
    pre = jnp.dot(rows, piece_in, preferred_element_type=jnp.float32)
    hidden = activate(pre).astype(jnp.bfloat16)
    part = jnp.dot(hidden, piece_out, preferred_element_type=jnp.float32).astype(jnp.bfloat16)
    returned = lax.all_to_all(
        part.reshape(-1, 1, features), "grp", split_axis=0, concat_axis=1, tiled=True
    )
    expert_sum = jnp.sum(
        returned.astype(jnp.float32).reshape(images, -1, 2, features), axis=2
    ).astype(jnp.bfloat16)
    output = (resid + mult("bne,bed->bnd", comb_low, expert_sum)).astype(jnp.bfloat16)
    again = (
        lax.all_gather(heads_in, "grp", axis=0, tiled=True),
        lax.all_gather(heads_out, "grp", axis=0, tiled=True),
        lax.all_gather(slot_router, "grp", axis=0, tiled=True),
        lax.all_gather(first_gain, "grp", axis=0, tiled=True),
        lax.all_gather(second_gain, "grp", axis=0, tiled=True),
    )
    back_in, back_out, back_router = (again[0], again[1], again[2])
    grad_comb = mult("bnd,bed->bne", cotangent, expert_sum)
    grad_sum = mult("bne,bnd->bed", comb_low, cotangent).astype(jnp.bfloat16)
    arriving = lax.all_to_all(
        jnp.repeat(grad_sum, 2, axis=1), "grp", split_axis=1, concat_axis=0, tiled=True
    ).reshape(-1, features)
    grad_hidden = mult("rd,hd->rh", arriving, piece_out)
    grad_piece_out = mult("rh,rd->hd", hidden, arriving)
    unused, gelu_back = jax.vjp(activate, pre)
    grad_pre = gelu_back(grad_hidden)[0].astype(jnp.bfloat16)
    grad_piece_in = mult("rd,rh->dh", rows, grad_pre)
    grad_rows = mult("rh,dh->rd", grad_pre, piece_in).astype(jnp.bfloat16)
    leaving = lax.all_to_all(
        grad_rows.reshape(-1, 1, features), "grp", split_axis=0, concat_axis=1, tiled=True
    )
    grad_slots = jnp.sum(
        leaving.astype(jnp.float32).reshape(images, -1, 2, features), axis=2
    ).astype(jnp.bfloat16)
    expert_in_term = grad_piece_in[None]
    expert_out_term = grad_piece_out[None]
    grad_disp = mult("bnd,bed->bne", act_two, grad_slots)
    grad_act_two = mult("bne,bed->bnd", disp_low, grad_slots)
    grad_logits = combine * (grad_comb - jnp.sum(grad_comb * combine, axis=2, keepdims=True))
    grad_logits = grad_logits + dispatch * (
        grad_disp - jnp.sum(grad_disp * dispatch, axis=1, keepdims=True)
    )
    grad_logits = grad_logits.astype(jnp.bfloat16)
    grad_router = mult("bnd,bne->de", act_two, grad_logits)
    grad_act_two = grad_act_two + mult("bne,de->bnd", grad_logits, back_router)
    grad_resid_norm, grad_gain_two = norm_back(grad_act_two, gain_two, normed_two, factor_two)
    grad_resid = cotangent.astype(jnp.float32) + grad_resid_norm
    grad_att = grad_resid.astype(jnp.bfloat16)
    grad_heads_out = mult("bnd,bne->de", mixed, grad_att)
    grad_mixed = mult("bne,de->bnd", grad_att, back_out).astype(jnp.bfloat16)
    grad_mixed = grad_mixed.reshape(images, places, head_count, head_size)
    again_scores = mult("bqhe,bkhe->bhqk", query, keys) * scaling
    prob_full = jnp.exp(again_scores - logsum)
    grad_values = mult("bhqk,bqhe->bkhe", prob_full.astype(jnp.bfloat16), grad_mixed)
    grad_probs = mult("bqhe,bkhe->bhqk", grad_mixed, values)
    grad_scores = prob_full * (grad_probs - jnp.sum(prob_full * grad_probs, axis=-1, keepdims=True))
    grad_scores = grad_scores.astype(jnp.bfloat16)
    grad_query = mult("bhqk,bkhe->bqhe", grad_scores, keys) * scaling
    grad_keys = mult("bhqk,bqhe->bkhe", grad_scores, query) * scaling
    grad_joint = jnp.stack([grad_query, grad_keys, grad_values], axis=2).reshape(
        images, places, 3 * features
    )
    grad_joint = grad_joint.astype(jnp.bfloat16)
    grad_heads_in = mult("bnd,bnf->df", act_one, grad_joint)
    grad_act_one = mult("bnf,df->bnd", grad_joint, back_in)
    grad_source, grad_gain_one = norm_back(grad_act_one, gain_one, normed_one, factor_one)
    token_grad = (grad_resid + grad_source).astype(jnp.bfloat16)
    rowed = (
        lax.psum_scatter(grad_heads_in, "grp", scatter_dimension=0, tiled=True),
        lax.psum_scatter(grad_heads_out, "grp", scatter_dimension=0, tiled=True),
        lax.psum_scatter(grad_router, "grp", scatter_dimension=0, tiled=True),
        lax.psum_scatter(grad_gain_one, "grp", scatter_dimension=0, tiled=True),
        lax.psum_scatter(grad_gain_two, "grp", scatter_dimension=0, tiled=True),
    )
    totals = lax.psum(
        (rowed[0], rowed[1], rowed[2], rowed[3], rowed[4], expert_in_term, expert_out_term), "rep"
    )
    shares = (totals[0], totals[1], totals[2], totals[3], totals[4])
    expert_in_grad, expert_out_grad = (totals[5], totals[6])
    return (
        output,
        token_grad,
        shares[0],
        shares[1],
        shares[2],
        shares[3],
        shares[4],
        expert_in_grad,
        expert_out_grad,
    )


def solution(mesh):
    in_specs = (
        P(("rep", "grp"), None, None),
        P(("rep", "grp"), None, None),
        P("grp", None),
        P("grp", None),
        P("grp", None),
        P("grp"),
        P("grp"),
        P("grp", None, None),
        P("grp", None, None),
    )
    out_specs = (
        P(("rep", "grp"), None, None),
        P(("rep", "grp"), None, None),
        P("grp", None),
        P("grp", None),
        P("grp", None),
        P("grp"),
        P("grp"),
        P("grp", None, None),
        P("grp", None, None),
    )
    return jax.shard_map(
        per_device, mesh=mesh, in_specs=in_specs, out_specs=out_specs, check_vma=False
    )
```

profile of v0, /device:TPU:0, one launch (start us, length us, event | category | flops | bytes accessed | tf_op | source)
XLA Modules:
  0.0 744.6 jit_solution(14243439978320597119)
XLA Ops:
  12.4 15.3 %all-reduce.7 = (bf16[768]{0:T(1024)(128)(2,1)S(1)}, bf16[768]{0:T(1024)(128)(2,1)S(1)}) all-reduce(bf16[768]{0:T(1024)(128)(2,1)S(1)} %dynamic-update-slice, bf16[768]{0:T(1024)(128)(2,1)S(1)} %dynamic-update-slice.1), channel_id=1, replica_groups=mesh['rep'=4,'grp'=8] {'grp'}, use_global_device_ids=true, to_apply=%add | all-reduce | flops 1536 | bytes 6144
  31.8 7.9 %all-gather = bf16[8,96,4]{1,2,0:T(4,128)(2,1)S(1)} all-gather(bf16[1,96,4]{1,2,0:T(4,128)(2,1)S(1)} %bitcast.164), channel_id=1, replica_groups=mesh['rep'=4,'grp'=8] {'grp'}, dimensions={0}, use_global_device_ids=true | all-gather | bytes 6912 | tf_op jit(solution)/shard_map/all_gather | solution.py:52
  39.8 6.9 all-gather.4.cloned.1.call-done
  46.7 9.8 %convolution_convert_fusion = bf16[6,197,2304]{2,1,0:T(8,128)(2,1)} fusion(bf16[768,2304]{1,0:T(8,128)(2,1)} %all-gather.4.cloned.1.call-done, bf16[6,197,768]{2,1,0:T(8,128)(2,1)} %param.9, f32[768]{0:T(1024)S(1)} %convert_element_type.89, f32[6,197]{1,0:T(8,128)S(1)} %add_rsqrt_fusion.1, f32[6,197]{1,0:T(8,128)S(1)} %broadcast_multiply_fusion.5), kind=kOutput, calls=%fused_computation.11 | convolution fusion | flops 4190294016 | bytes 10813680 | tf_op jit(solution)/shard_map/bnd,df->bnf/dot_general | solution.py:10
  56.5 9.2 %copy.47 = bf16[6,197,2304]{1,2,0:T(8,128)(2,1)} copy(bf16[6,197,2304]{2,1,0:T(8,128)(2,1)} %convolution_convert_fusion) | data formatting | bytes 10893312 | tf_op jit(solution)/shard_map/convert_element_type | solution.py:62
  65.7 9.8 %multiply_reduce_fusion.1 = (f32[6,12,197]{2,1,0:T(8,128)S(1)}, f32[6,12,197,197]{2,3,1,0:T(8,128)}) fusion(bf16[6,197,3,12,64]{1,4,3,2,0:T(8,128)(2,1)} %bitcast.147), kind=kOutput, calls=%fused_computation.8 | convolution fusion | flops 363238048 | bytes 15952320 | tf_op jit(solution)/shard_map/bqhe,bkhe->bhqk/dot_general | solution.py:10
  75.5 8.8 %exponential_reduce_fusion = f32[6,12,197]{2,1,0:T(8,128)S(1)} fusion(f32[6,12,197,197]{2,3,1,0:T(8,128)} %get-tuple-element.29, f32[6,12,197]{2,1,0:T(8,128)S(1)} %get-tuple-element.28), kind=kLoop, calls=%fused_computation.7 | loop fusion | flops 8368560 | bytes 11290464 | tf_op jit(solution)/shard_map/reduce_sum | solution.py:67
  84.3 10.2 %fusion.35 = bf16[6,12,64,197]{3,2,1,0:T(8,128)(2,1)} fusion(bf16[6,197,3,12,64]{1,4,3,2,0:T(8,128)(2,1)} %bitcast.148, f32[6,12,197,197]{2,3,1,0:T(8,128)} %get-tuple-element.29, f32[6,12,197]{2,1,0:T(8,128)S(1)} %log_add_fusion), kind=kOutput, calls=%fused_computation.64 | convolution fusion | flops 366954272 | bytes 18977184 | tf_op jit(solution)/shard_map/bhqk,bkhe->bqhe/dot_general | solution.py:10
  117.6 5.1 all-to-all-done.2
  148.1 6.7 multiply_reduce_fusion.2
  154.7 5.0 multiply_add_fusion
  164.7 5.3 convolution_convert_fusion.1
  174.0 15.6 %multiply_reduce_fusion = (f32[6,12,197]{2,1,0:T(8,128)S(1)}, f32[6,12,197,197]{2,3,1,0:T(8,128)}) fusion(f32[6,12,197,197]{2,3,1,0:T(8,128)} %get-tuple-element.29, f32[6,12,197]{2,1,0:T(8,128)S(1)} %log_add_fusion, bf16[6,197,12,64]{1,3,2,0:T(8,128)(2,1)} %bitcast.152, bf16[6,197,3,12,64]{1,4,3,2,0:T(8,128)(2,1)} %bitcast.149), kind=kOutput, calls=%fused_computation.5 | convolution fusion | flops 368826528 | bytes 30754656 | tf_op jit(solution)/shard_map/bqhe,bkhe->bhqk/dot_general | solution.py:10
  189.6 10.7 %multiply_convert_fusion = bf16[6,12,197,197]{2,3,1,0:T(8,128)(2,1)S(1)} fusion(f32[6,12,197,197]{2,3,1,0:T(8,128)} %get-tuple-element.38, f32[6,12,197,197]{2,3,1,0:T(8,128)} %get-tuple-element.29, f32[6,12,197]{2,1,0:T(8,128)S(1)} %get-tuple-element.37, f32[6,12,197]{2,1,0:T(8,128)S(1)} %log_add_fusion), kind=kLoop, calls=%fused_computation.4 | loop fusion | flops 13971240 | bytes 28055952 | tf_op jit(solution)/shard_map/convert_element_type | solution.py:146
  208.0 6.4 fusion.23
  214.4 8.9 %convert_bitcast_fusion = bf16[6,197,1,12,64]{1,4,3,0,2:T(8,128)(2,1)S(1)} fusion(bf16[6,197,12,64]{1,3,2,0:T(8,128)(2,1)S(1)} %bitcast.153, f32[6,12,197,197]{2,3,1,0:T(8,128)} %get-tuple-element.29, f32[6,12,197]{2,1,0:T(8,128)S(1)} %log_add_fusion), kind=kOutput, calls=%fused_computation.59 | convolution fusion | flops 366954272 | bytes 14864832 | tf_op jit(solution)/shard_map/bhqk,bqhe->bkhe/dot_general | solution.py:10
  230.3 11.8 %convolution_bitcast_fusion = f32[768,2304]{1,0:T(8,128)} fusion(bf16[6,197,2304]{1,2,0:T(8,128)(2,1)} %bitcast.154, bf16[6,197,768]{2,1,0:T(8,128)(2,1)S(1)} %copy-done.7, f32[768]{0:T(1024)S(1)} %convert_element_type.89, f32[6,197]{1,0:T(8,128)S(1)} %add_rsqrt_fusion.1, f32[6,197]{1,0:T(8,128)S(1)} %broadcast_multiply_fusion.5), kind=kOutput, calls=%fused_computation.12 | convolution fusion | flops 4187570688 | bytes 14352624 | tf_op jit(solution)/shard_map/bnd,bnf->df/dot_general | solution.py:10
  251.1 69.3 %reduce-scatter.6.cloned.1.call-done = f32[96,2304]{1,0:T(8,128)} async-done(((f32[768,2304]{1,0:T(8,128)}), f32[96,2304]{1,0:T(8,128)}) %reduce-scatter.6.cloned.1.call-update) | async-done | bytes 884752 | tf_op jit(solution)/shard_map/reduce_scatter | solution.py:158
  321.9 12.4 %fusion.17 = (f32[768]{0:T(1024)S(1)}, f32[6,197]{1,0:T(8,128)S(1)}, f32[6,197]{1,0:T(8,128)S(1)}, f32[6,197,768]{2,1,0:T(8,128)}) fusion(bf16[6,197,768]{2,1,0:T(8,128)(2,1)S(1)} %copy-done.8, f32[6,197]{1,0:T(8,128)S(1)} %add_rsqrt_fusion.1, f32[6,197]{1,0:T(8,128)S(1)} %broadcast_multiply_fusion.5, f32[768]{0:T(1024)S(1)} %convert_element_type.89, ...), kind=kOutput, calls=%fused_computation.32 | convolution fusion | flops 4191198464 | bytes 14457312 | tf_op jit(solution)/shard_map/bnf,df->bnd/dot_general | solution.py:10
  334.4 13.0 %all-reduce.4 = (f32[768]{0:T(1024)S(1)}, f32[768]{0:T(1024)S(1)}) all-reduce(f32[768]{0:T(1024)S(1)} %get-tuple-element.11, f32[768]{0:T(1024)S(1)} %get-tuple-element.9), channel_id=5, replica_groups=mesh['rep'=4,'grp'=8] {'grp'}, use_global_device_ids=true, to_apply=%region_26.0.clone | all-reduce | flops 1536 | bytes 12288
  351.6 4.8 fusion.16
  358.6 12.4 %all-reduce.5 = (f32[96,4]{0,1:T(4,128)}, f32[96]{0:T(128)}, f32[96]{0:T(128)}) all-reduce(f32[96,4]{0,1:T(4,128)S(1)} %copy.79, f32[96]{0:T(128)S(1)} %dynamic-slice.3, f32[96]{0:T(128)S(1)} %dynamic-slice.5), channel_id=1, replica_groups=mesh['rep'=4,'grp'=8] {'rep'}, use_global_device_ids=true, to_apply=%region_24.0 | all-reduce | flops 576 | bytes 4608 | tf_op jit(solution)/shard_map/psum | solution.py:164
  371.0 355.4 %all-reduce.10.cloned.1.call-done = (f32[96,2304]{1,0:T(8,128)}, f32[96,768]{1,0:T(8,128)}, f32[1,768,1536]{2,1,0:T(8,128)}, f32[1,1536,768]{2,1,0:T(8,128)}) async-done(((f32[96,2304]{1,0:T(8,128)}, f32[96,768]{1,0:T(8,128)}, f32[1,768,1536]{2,1,0:T(8,128)}, f32[1,1536,768]{2,1,0:T(8,128)}), (f32[96,2304]{1,0:T(8,128)}, f32[96,768]{1,0:T(8,128)}, f32[1,768,1536]{2,1,0:T(8,128)}, ...) | async-done | bytes 10616848 | tf_op jit(solution)/shard_map/psum | solution.py:164
  730.3 5.0 copy.105
  (136 shorter events, 102.8 us)
Async XLA Ops:
  7.2 115.5 %copy-start = (bf16[1,768,1536]{2,1,0:T(8,128)(2,1)S(1)}, bf16[1,768,1536]{2,1,0:T(8,128)(2,1)}, u32[]{:S(2)}) copy-start(bf16[1,768,1536]{2,1,0:T(8,128)(2,1)} %param.16) | copy-start | bytes 7077892
  7.2 24.6 %copy-start.19 = (bf16[96,4]{0,1:T(4,128)(2,1)S(1)}, bf16[96,4]{0,1:T(4,128)(2,1)}, u32[]{:S(2)}) copy-start(bf16[96,4]{0,1:T(4,128)(2,1)} %param.13) | copy-start | bytes 2308
  7.2 39.5 %all-gather.4.cloned.1.call-start = ((), (), s32[]{:S(2)}) async-start(), calls=%async_computation.7 | async-start | bytes 3981312 | tf_op jit(solution)/shard_map/all_gather | solution.py:50
  7.9 86.6 %all-gather.6.cloned.1.call-start = ((), (), s32[]{:S(2)}) async-start(), calls=%async_computation.8 | async-start | bytes 1327104 | tf_op jit(solution)/shard_map/all_gather | solution.py:51
  102.2 45.8 %copy-start.17 = (f32[6,197,4]{1,2,0:T(4,128)}, f32[6,197,4]{1,2,0:T(4,128)S(1)}, u32[]{:S(2)}) copy-start(f32[6,197,4]{1,2,0:T(4,128)S(1)} %get-tuple-element.35) | copy-start | bytes 56740
  104.8 8.7 %all-to-all-start = ((bf16[6,8,768]{2,0,1:T(8,128)(2,1)}), bf16[6,8,768]{2,0,1:T(8,128)(2,1)S(1)}, u32[]{:S(2)}, u32[]{:S(2)}) async-start(bf16[6,8,768]{2,0,1:T(8,128)(2,1)} %bitcast.10), calls=%async_computation | async-start | bytes 196608 | tf_op jit(solution)/shard_map/all_to_all | solution.py:83
  114.2 8.5 %all-to-all-start.2 = ((bf16[6,8,768]{2,0,1:T(8,128)(2,1)}), bf16[6,8,768]{2,0,1:T(8,128)(2,1)S(1)}, u32[]{:S(2)}, u32[]{:S(2)}) async-start(bf16[6,8,768]{2,0,1:T(8,128)(2,1)} %bitcast.18), calls=%async_computation.2 | async-start | bytes 196608 | tf_op jit(solution)/shard_map/all_to_all | solution.py:109
  117.6 9.1 %copy-start.11 = (bf16[48,768]{1,0:T(8,128)(2,1)}, bf16[48,768]{1,0:T(8,128)(2,1)S(1)}, u32[]{:S(2)}) copy-start(bf16[48,768]{1,0:T(8,128)(2,1)S(1)} %reshape.112) | copy-start | bytes 221188
  125.9 18.0 %copy-start.13 = (bf16[48,1536]{1,0:T(8,128)(2,1)}, bf16[48,1536]{1,0:T(8,128)(2,1)S(1)}, u32[]{:S(2)}) copy-start(bf16[48,1536]{1,0:T(8,128)(2,1)S(1)} %fusion.72) | copy-start | bytes 442372
  128.5 8.4 %all-to-all-start.3 = ((bf16[8,2,2304]{2,1,0:T(2,128)(2,1)}), bf16[8,2,2304]{2,1,0:T(2,128)(2,1)S(1)}, u32[]{:S(2)}, u32[]{:S(2)}) async-start(bf16[8,2,2304]{2,1,0:T(2,128)(2,1)} %reshape.145), calls=%async_computation.3 | async-start | bytes 147456 | tf_op jit(solution)/shard_map/all_to_all | solution.py:118
  131.9 12.0 %copy-start.5 = (bf16[6,197,768]{2,1,0:T(8,128)(2,1)S(1)}, bf16[6,197,768]{2,1,0:T(8,128)(2,1)}, u32[]{:S(2)}) copy-start(bf16[6,197,768]{2,1,0:T(8,128)(2,1)} %copy-done.4) | copy-start | bytes 5446660
  136.9 8.4 %all-to-all-start.1 = ((bf16[8,2,2304]{2,1,0:T(2,128)(2,1)}), bf16[8,2,2304]{2,1,0:T(2,128)(2,1)S(1)}, u32[]{:S(2)}, u32[]{:S(2)}) async-start(bf16[8,2,2304]{2,1,0:T(2,128)(2,1)} %reshape.143), calls=%async_computation.1 | async-start | bytes 147456 | tf_op jit(solution)/shard_map/all_to_all | solution.py:92
  140.3 110.8 %reduce-scatter.8.cloned.1.call-start = ((), (), s32[]{:S(2)}) async-start(), calls=%async_computation.10 | async-start | bytes 2654208 | tf_op jit(solution)/shard_map/reduce_scatter | solution.py:159
  154.7 6.8 copy-start.10
  207.8 112.6 %reduce-scatter.6.cloned.1.call-start = ((), (), s32[]{:S(2)}) async-start(), calls=%async_computation.9 | async-start | bytes 7962624 | tf_op jit(solution)/shard_map/reduce_scatter | solution.py:158
  208.0 6.4 copy-start.6
  242.1 3.9 copy-start.18
  242.1 5.8 copy-start.12
  242.1 5.8 copy-start.14
  242.2 115.6 %reduce-scatter.10.cloned.1.call-start = ((), (), s32[]{:S(2)}) async-start(), calls=%async_computation.11 | async-start | bytes 442368
  247.6 478.7 %all-reduce.10.cloned.1.call-start = ((), (), s32[]{:S(2)}) async-start(), calls=%async_computation.12 | async-start | bytes 21233664 | tf_op jit(solution)/shard_map/psum | solution.py:164
  728.5 6.9 slice-start
  730.3 5.0 slice-start.1
  730.3 7.2 copy-start.1
  (8 other events, 14.5 us)
Sparse Core Ops, SparseCore 0:
  9.9 36.7 all-gather.3
  48.6 24.0 all-gather.5
  207.9 43.1 reduce-scatter.7
  254.9 65.4 reduce-scatter.5
  323.9 33.8 reduce-scatter.9
  361.7 364.6 all-reduce.9
where the time goes:
time: 751 us; the launch traced here: 745 us
  waiting for transfers between devices  445 us (59%)
  matrix products  137 us (18%)
  blocking collectives  48.7 us (6%)
  local copies, waits for them, and re-layouts  43.4 us (6%)
  other arithmetic  40.3 us (5%)
  between operations  16.3 us (2%)
  starting transfers between devices  14.3 us (2%)
    psum x1, waiting for transfers between devices, per_device(): lax.psum((rowed[0], rowed[1], rowed[2], rowed[3], rowed[4], expert_in_ter...  355 us
    dot_general x25, matrix products, mult(): return jnp.einsum(form, left, right, preferred_element_type=jnp.float32)  134 us
    reduce_scatter x1, waiting for transfers between devices, per_device(): lax.psum_scatter(grad_heads_in, 'grp', scatter_dimension=0, tiled=True)  69.3 us
    unnamed x2, blocking collectives  28.4 us
    unnamed x61, local copies, waits for them, and re-layouts  24.6 us
  transfers between devices with their start and end apart: 10, of which 9 were waited for; matrix products, arithmetic and copies ran while one was open for 17% of the time, Pallas kernels for 0%

commit v1 on v0

v1 whole, which is shorter than its diff:
```python
import functools

import jax
import jax.numpy as jnp
from jax import lax
from jax.experimental import pallas as pl
from jax.experimental.pallas import tpu as pltpu
from jax.sharding import PartitionSpec as P

HEADS = 12
LANES = 128
F32 = jnp.float32
BF16 = jnp.bfloat16
LOW = -1e30

NN = (((1,), (0,)), ((), ()))
NT = (((1,), (1,)), ((), ()))
TN = (((0,), (0,)), ((), ()))


def dot(left, right, form=NN):
    return lax.dot_general(left, right, form, preferred_element_type=F32)


def swap(values, axis, size, bit):
    return lax.ppermute(values, axis, [(place, place ^ bit) for place in range(size)])


def after(values, *others):
    return lax.optimization_barrier((values, others))[0]


def gather_first(own):
    return swap(own[0], "grp", 8, 2), swap(own[1], "grp", 8, 4)


def gather_second(joined):
    return swap(joined[0], "grp", 8, 4), swap(joined[1], "grp", 8, 2)


def gather_last(*stages):
    held = tuple(part for stage in stages for part in stage)
    return held + tuple(swap(part, "grp", 8, 1) for part in held)


def as_gathered(blocks, cut):
    held = []
    for k in range(2):
        own, x, y, far = blocks[k], blocks[k + 2], blocks[k + 4], blocks[k + 6]
        held += [own[:cut], own[cut:], x[:cut], y[cut:]]
        held += [jnp.concatenate([y[:cut], far[:cut]]), jnp.concatenate([x[cut:], far[cut:]])]
    return tuple(held)


def iota(shape, axis):
    return lax.broadcasted_iota(jnp.int32, shape, axis)


def normalize(values):
    center = values - jnp.mean(values, axis=-1, keepdims=True)
    factor = lax.rsqrt(jnp.mean(center * center, axis=-1, keepdims=True) + 1e-06)
    return center * factor, factor


def norm_back(scaled, normed, factor):
    inner = (
        scaled
        - jnp.mean(scaled, axis=-1, keepdims=True)
        - normed * jnp.mean(scaled * normed, axis=-1, keepdims=True)
    )
    return factor * inner


def pieces_of(rows, extra):
    half = rows // 2
    cut = extra + half
    for core in range(2):
        base = 6 * core
        yield base, extra, core, 0
        yield base + 1, 0, core, half
        yield base + 2, extra, core + 2, 0
        yield base + 3, 0, core + 4, half
        yield base + 4, extra, core + 4, 0
        yield base + 4, cut + extra, core + 6, 0
        yield base + 5, 0, core + 2, half
        yield base + 5, half, core + 6, half


def place_pieces(order_ref, pieces, rows, extra, target, columns):
    half = rows // 2
    for n, start, block, offset in pieces_of(rows, extra):
        place = pl.multiple_of(order_ref[block] * rows + offset, 16)
        target[pl.ds(place, half), :] = pieces[n][start : start + half, columns]


def store_blocks(order_ref, source, targets, columns):
    rows = source.shape[0] // 8
    n = 0
    for target in targets:
        for k in range(target.shape[0] // rows):
            start = pl.multiple_of(order_ref[8 + n] * rows, 32)
            target[k * rows : (k + 1) * rows, columns] = source[pl.ds(start, rows), :].astype(BF16)
            n += 1


def gather_small(order_ref, pieces, rows, extra, small_ref):
    total = jnp.zeros(small_ref.shape, F32)
    lane = iota((LANES, small_ref.shape[1]), 0)
    place = iota((LANES, small_ref.shape[1]), 1)
    cut = extra + rows // 2
    for core in range(2):
        for n, start, block in ((0, 0, 0), (2, 0, 2), (4, 0, 4), (4, cut, 6)):
            held = pieces[6 * core + n][start : start + extra, :LANES]
            fits = (place == order_ref[block + core] * rows + lane) & (lane < rows)
            total = total + dot(held, jnp.where(fits, 1.0, 0.0).astype(BF16))
    small_ref[...] = total


def rows_of(place, tall):
    return pl.ds(pl.multiple_of(place * tall, 16), tall)


VM = pl.BlockSpec(memory_space=pltpu.VMEM)
SM = pl.BlockSpec(memory_space=pltpu.SMEM)


def call(body, name, inputs, outputs, scratch, limit, flops, hbm=()):
    return pl.pallas_call(
        body,
        in_specs=[SM if x.dtype == jnp.int32 else VM for x in inputs],
        out_specs=[VM] * len(outputs),
        out_shape=[
            jax.ShapeDtypeStruct(shape, kind) if n in hbm else pltpu.VMEM(shape, kind)
            for n, (shape, kind) in enumerate(outputs)
        ],
        scratch_shapes=[pltpu.VMEM(shape, kind) for shape, kind in scratch],
        compiler_params=pltpu.CompilerParams(vmem_limit_bytes=limit * 1024 * 1024),
        cost_estimate=pl.CostEstimate(flops=int(flops), bytes_accessed=1000000, transcendentals=0),
        name=name,
    )(*inputs)


def prepare_body(in_ref, out_ref, router_ref, gains_ref, h0, h1, t0, t1):
    rows, features = out_ref.shape
    half = rows // 2
    experts = router_ref.shape[1]
    part = features // 3
    extra = h0.shape[0] - half
    gains = gains_ref[...].astype(F32)
    router = router_ref[...].astype(F32)
    router = jnp.concatenate([router, jnp.zeros((rows, LANES - experts), F32)], axis=1).T
    small = jnp.concatenate([gains, router[: extra - 2]], axis=0)
    small = jnp.concatenate([small, jnp.zeros((extra, LANES - rows), F32)], axis=1)
    h0[:extra, :] = jnp.zeros((extra, h0.shape[1]), BF16)
    h0[:extra, :LANES] = small.astype(BF16)
    for head, tail, start, here in ((h0, t0, extra, slice(0, half)), (h1, t1, 0, slice(half, rows))):
        for k in range(3):
            base = k * features
            head[start:, k * part : (k + 1) * part] = in_ref[here, base : base + part]
            tail[:, 2 * k * part : 2 * (k + 1) * part] = in_ref[here, base + part : base + features]
        tail[:, 2 * features :] = out_ref[here, :]


def prepare(heads_in, heads_out, router, gains):
    rows, features = heads_out.shape
    extra = -(-(router.shape[1] + 2) // 16) * 16
    return call(
        prepare_body,
        "prepare",
        (heads_in, heads_out, router, gains),
        [
            ((extra + rows // 2, features), BF16),
            ((rows // 2, features), BF16),
            ((rows // 2, 3 * features), BF16),
            ((rows // 2, 3 * features), BF16),
        ],
        [],
        4,
        1e6,
    )


def join_body(a0, a1, b0, b1, a_ref, b_ref):
    for first, second, target in ((a0, a1, a_ref), (b0, b1, b_ref)):
        target[: first.shape[0], :] = first[...]
        target[first.shape[0] :, :] = second[...]


def join(own, got):
    outputs = [((2 * x.shape[0], x.shape[1]), BF16) for x in own]
    return call(join_body, "join", (own[0], got[0], own[1], got[1]), outputs, [], 4, 1e6)


def attend_body(first, images, places, order_ref, source_ref, *refs):
    pieces, refs = refs[:12], refs[12:]
    features = source_ref.shape[1]
    rows = features // 8
    if first:
        act_ref, small_ref, weight, joint_ref, prob_ref, mixed_ref = refs
        extra = small_ref.shape[0]
    else:
        out_weight, weight, joint_ref, prob_ref, mixed_ref = refs
        act_ref = source_ref
        extra = 0
    tall = source_ref.shape[0] // images
    width = weight.shape[1]
    place_pieces(order_ref, pieces, rows, extra, weight, slice(0, width))
    if first:
        gather_small(order_ref, pieces, rows, extra, small_ref)

        @pl.loop(0, images)
        def _(i):
            here = rows_of(i, tall)
            normed, _ = normalize(source_ref[here, :].astype(F32))
            act_ref[here, :] = (normed * small_ref[0:1, :]).astype(BF16)
    else:
        place_pieces(order_ref, pieces, rows, 0, out_weight, slice(width, width + features))

    @pl.loop(0, images // 2)
    def _(i):
        here = rows_of(i, 2 * tall)
        joint_ref[here, :] = dot(act_ref[here, :], weight[...]).astype(BF16)

    third = width // 3
    heads = prob_ref.shape[0] // images
    low = iota((tall, LANES), 1) < LANES // 2
    inside = iota((tall, LANES), 0) < places
    seen = iota((tall, tall), 1) < places

    @pl.loop(0, images)
    def _(i):
        here = rows_of(i, tall)
        for pair in range(third // LANES):
            query, keys, values = (
                joint_ref[here, part * third + pair * LANES : part * third + (pair + 1) * LANES]
                for part in range(3)
            )
            query = query * 0.125
            outs = []
            for side in range(2):
                mine = low if side == 0 else ~low
                scores = dot(jnp.where(mine, query, 0), keys, NT)
                scores = jnp.where(seen, scores, LOW)
                power = jnp.exp(scores - jnp.max(scores, axis=1, keepdims=True))
                prob = (power * (1.0 / jnp.sum(power, axis=1, keepdims=True))).astype(BF16)
                prob_ref[i * heads + 2 * pair + side] = prob
                outs.append(dot(prob, values))
            mixed = jnp.where(inside, jnp.where(low, outs[0], outs[1]), 0.0)
            mixed_ref[here, pair * LANES : (pair + 1) * LANES] = mixed.astype(BF16)


def attend(first, images, places, order, source, pieces, width):
    total, features = source.shape
    tall = total // images
    heads = width // 3 // 64
    extra = pieces[0].shape[0] - features // 16
    outputs = [
        ((features, width), BF16),
        ((total, width), BF16),
        ((images * heads, tall, tall), BF16),
        ((total, width // 3), BF16),
    ]
    if first:
        outputs = [((total, features), BF16), ((extra, features), F32)] + outputs
    else:
        outputs = [((features, features), BF16)] + outputs
    return call(
        functools.partial(attend_body, first, images, places),
        "attend",
        (order, source, *pieces),
        outputs,
        [],
        12,
        2 * total * features * width * 2,
    )


def softmaxes(logits, places, experts):
    rows = iota(logits.shape, 0) < experts
    lanes = iota(logits.shape, 1) < places
    wide = jnp.where(lanes, logits, LOW)
    wide = jnp.exp(wide - jnp.max(wide, axis=1, keepdims=True))
    dispatch = wide / jnp.sum(wide, axis=1, keepdims=True)
    tall = jnp.where(rows, logits, LOW)
    tall = jnp.exp(tall - jnp.max(tall, axis=0, keepdims=True))
    combine = tall / jnp.sum(tall, axis=0, keepdims=True)
    return jnp.where(rows, dispatch, 0.0), combine


def slot_rows_of(experts, order_ref, small_ref, slots):
    rows = small_ref.shape[0]
    slot, row = iota((slots, rows), 0), iota((slots, rows), 1)
    chip = order_ref[order_ref.shape[0] - 1]
    fits = (row == (slot ^ chip) + 2) & (slot < experts)
    return dot(jnp.where(fits, 1.0, 0.0).astype(BF16), small_ref[...].astype(BF16)).astype(BF16)


def pick_rows(shape, wanted):
    row, column = iota(shape, 0), iota(shape, 1)
    return jnp.where(column == wanted(row), 1.0, 0.0).astype(BF16)


def route_body(
    images, places, experts, order_ref, token_ref, cot_ref, m0, m1, weight, small_ref,
    resid_ref, logit_ref, *refs,
):
    out_refs, packed_ref = refs[:-1], refs[-1]
    slots = logit_ref.shape[0] // images
    router = slot_rows_of(experts, order_ref, small_ref, slots)
    tall = token_ref.shape[0] // images
    features = token_ref.shape[1]

    @pl.loop(0, images // 2)
    def _(i):
        here = rows_of(i, 2 * tall)
        mixed = jnp.concatenate([m0[here, :], m1[here, :]], axis=1)
        resid_ref[here, :] = token_ref[here, :].astype(F32) + dot(mixed, weight[...])

    @pl.loop(0, images)
    def _(i):
        here = rows_of(i, tall)
        normed, _ = normalize(resid_ref[here, :])
        act = (normed * small_ref[1:2, :]).astype(BF16)
        logits = dot(router, act, NT)
        group = rows_of(i, slots)
        logit_ref[group, :] = logits
        dispatch, combine = softmaxes(logits, places, experts)
        packed_ref[group, :features] = dot(dispatch.astype(BF16), act).astype(BF16)
        packed_ref[group, features:] = dot(combine.astype(BF16), cot_ref[here, :]).astype(BF16)

    high = out_refs[0].shape[0]
    pick = pick_rows(
        (experts * high, images * slots),
        lambda n: jnp.where(n % high < images, n % high * slots + n // high, -1),
    )
    packed = dot(pick, packed_ref[...]).astype(BF16)
    for k, out_ref in enumerate(out_refs):
        out_ref[...] = packed[k * high : (k + 1) * high, :]


def route(images, places, experts, slots, order, tokens, cot, mixed, w, small):
    total, features = tokens.shape
    high = -(-images // 8) * 8
    return call(
        functools.partial(route_body, images, places, experts),
        "route",
        (order, tokens, cot, *mixed, w, small),
        [((total, features), F32), ((images * slots, total // images), F32)]
        + [((high, 2 * features), BF16)] * experts,
        [((images * slots, 2 * features), BF16)],
        10,
        4 * total * features * features,
    )


def gelu_parts(values):
    scale, cubic = 0.7978845608028654, 0.044715
    square = values * values
    bent = jnp.tanh(scale * values * (1.0 + cubic * square))
    half = 0.5 * (1.0 + bent)
    slope = half + 0.5 * values * (1.0 - bent * bent) * scale * (1.0 + 3.0 * cubic * square)
    return values * half, slope


def expert_body(count, images, in_ref, out_ref, *refs):
    sources, (packed_ref, keep_ref, give_ref, rows_ref, back_ref) = refs[:count], refs[count:]
    features = in_ref.shape[0]
    high = sources[0].shape[0]
    for k, source in enumerate(sources):
        rows_ref[k * high : (k + 1) * high, :] = source[...]
    rows, arriving = rows_ref[:, :features], rows_ref[:, features:]
    total = jnp.zeros((rows.shape[0], features), F32)
    grad_total = total
    step = 512
    for start in range(0, in_ref.shape[1], step):
        w_in = in_ref[:, start : start + step]
        w_out = out_ref[start : start + step, :]
        hidden, slope = gelu_parts(dot(rows, w_in))
        grad_pre = (dot(arriving, w_out, NT) * slope).astype(BF16)
        total = total + dot(hidden.astype(BF16), w_out)
        grad_total = grad_total + dot(grad_pre, w_in, NT)
    back_ref[:, :features] = total.astype(BF16)
    back_ref[:, features:] = grad_total.astype(BF16)
    half = keep_ref.shape[0]
    keep_ref[...] = back_ref[:half, :]
    give_ref[...] = back_ref[half:, :]
    pick = pick_rows(
        (packed_ref.shape[0], rows_ref.shape[0]), lambda n: n // images * high + n % images
    )
    packed_ref[...] = dot(pick, rows_ref[...]).astype(BF16)


def expert(images, piece_in, piece_out, sources):
    high, wide = sources[0].shape
    rows = high * len(sources)
    return call(
        functools.partial(expert_body, len(sources), images),
        "expert",
        (piece_in, piece_out, *sources),
        [
            ((images * len(sources), wide), BF16),
            ((rows // 2, wide), BF16),
            ((rows // 2, wide), BF16),
        ],
        [((rows, wide), BF16)] * 2,
        8,
        1e9,
    )


def pair_sum_body(parts, keep_ref, *refs):
    got_refs, out_refs = refs[:parts], refs[parts:]
    rows = out_refs[0].shape[0]
    each = len(out_refs) // parts
    for k, out_ref in enumerate(out_refs):
        kept = keep_ref[k * rows : (k + 1) * rows, :].astype(F32)
        got = got_refs[k // each][k % each * rows : (k % each + 1) * rows, :].astype(F32)
        out_ref[...] = (kept + got).astype(BF16)


def pair_sum(keep, got, count):
    shape = (keep.shape[0] // count, keep.shape[1])
    body = functools.partial(pair_sum_body, len(got))
    return call(body, "pair_sum", (keep, *got), [(shape, BF16)] * count, [], 4, 1e6)


def total_body(*refs):
    refs[-1][...] = sum(ref[...].astype(F32) for ref in refs[:-1]).astype(BF16)


def total_sum(*terms):
    return call(total_body, "total_sum", terms, [(terms[0].shape, BF16)], [], 4, 1e6)[0]


def split_sum_body(order_ref, *refs):
    terms, (mine_ref, give_ref, scratch) = refs[:-3], refs[-3:]
    scratch[...] = sum(ref[...].astype(F32) for ref in terms)
    half = mine_ref.shape[0]
    odd = order_ref[order_ref.shape[0] - 2]
    mine = pl.multiple_of(odd * half, 16)
    other = pl.multiple_of((1 - odd) * half, 16)
    mine_ref[...] = scratch[pl.ds(mine, half), :].astype(BF16)
    give_ref[...] = scratch[pl.ds(other, half), :].astype(BF16)


def split_sum(order, *terms):
    rows, wide = terms[0].shape
    shape = (rows // 2, wide)
    return call(
        split_sum_body, "split_sum", (order, *terms), [(shape, BF16)] * 2, [((rows, wide), F32)], 8, 1e6
    )


def shares_body(
    experts, order_ref, head_ref, head_other, tail_ref, tail_other, w_ref, gain_ref,
    in_ref, out_ref, router_ref, gain_one_ref, gain_two_ref, tail,
):
    rows, features = out_ref.shape
    half = rows // 2
    odd = order_ref[order_ref.shape[0] - 2]
    tail[pl.ds(pl.multiple_of(odd * half, 16), half), :] = tail_ref[...].astype(F32)
    tail[pl.ds(pl.multiple_of((1 - odd) * half, 16), half), :] = tail_other[...].astype(F32)
    part = features // 3
    for k in range(3):
        here = slice(k * part, (k + 1) * part)
        in_ref[:, k * features : k * features + part] = (
            head_ref[:, here].astype(F32) + head_other[:, here].astype(F32)
        )
        in_ref[:, k * features + part : (k + 1) * features] = tail[:, 2 * k * part : 2 * (k + 1) * part]
    out_ref[...] = tail[:, 2 * features : 3 * features]
    rest = tail[:, 3 * features :]
    router_ref[...] = rest[:, :experts]
    gain_two_ref[...] = rest.T[experts : experts + 1, :]
    gain_one = jnp.sum(in_ref[...] * w_ref[...].astype(F32), axis=1, keepdims=True)
    gain_one = jnp.broadcast_to(gain_one, (rows, LANES)).T[:1, :]
    gain_one_ref[...] = gain_one / gain_ref[...].astype(F32)


def shares(experts, order, head, head_other, tail, tail_other, w, gain):
    rows, features = head.shape
    return call(
        functools.partial(shares_body, experts),
        "shares",
        (order, head, head_other, tail, tail_other, w, gain),
        [
            (w.shape, F32),
            ((rows, features), F32),
            ((rows, experts), F32),
            ((1, rows), F32),
            ((1, rows), F32),
        ],
        [((rows, tail.shape[1]), F32)],
        8,
        1e6,
        hbm=range(5),
    )


def expert_grad_body(count, *refs):
    sources, (in_ref, out_ref, grad_in_ref, grad_out_ref) = refs[:count], refs[count:]
    features = in_ref.shape[0]
    every = jnp.concatenate([source[...] for source in sources], axis=0)
    rows, arriving = every[:, :features], every[:, features:]
    hidden, slope = gelu_parts(dot(rows, in_ref[...]))
    grad_pre = (dot(arriving, out_ref[...], NT) * slope).astype(BF16)
    grad_in_ref[...] = dot(rows, grad_pre, TN)
    grad_out_ref[...] = dot(hidden.astype(BF16), arriving, TN)


def expert_grad(sources, piece_in, piece_out):
    features, hidden = piece_in.shape
    step = 256
    wide = pl.BlockSpec((features, step), lambda i: (0, i))
    high = pl.BlockSpec((step, features), lambda i: (i, 0))
    return pl.pallas_call(
        functools.partial(expert_grad_body, len(sources)),
        grid=(hidden // step,),
        in_specs=[pl.BlockSpec(x.shape, lambda i: (0, 0)) for x in sources] + [wide, high],
        out_specs=[wide, high],
        out_shape=[
            jax.ShapeDtypeStruct(piece_in.shape, F32),
            jax.ShapeDtypeStruct(piece_out.shape, F32),
        ],
        compiler_params=pltpu.CompilerParams(vmem_limit_bytes=16 * 1024 * 1024),
        cost_estimate=pl.CostEstimate(
            flops=1600 * piece_in.size, bytes_accessed=14000000, transcendentals=0
        ),
        name="expert_grad",
    )(*sources, piece_in, piece_out)


def back_body(
    images, places, experts, order_ref, resid_ref, logit_ref, cot_ref, m0, m1, weight, small_ref, *refs
):
    sources, refs = refs[:experts], refs[experts:]
    output_ref, att_ref, grad_mixed_ref, grad_w_ref, grad_side_ref, summed_ref = refs
    slots = logit_ref.shape[0] // images
    router = slot_rows_of(experts, order_ref, small_ref, slots)
    total, features = resid_ref.shape
    tall = total // images
    gain = small_ref[1:2, :]
    high = sources[0].shape[0]
    pick = pick_rows(
        (images * slots, experts * high),
        lambda n: jnp.where(n % slots < experts, n % slots * high + n // slots, -1),
    )
    arrived = jnp.concatenate([source[...] for source in sources], axis=0)
    summed_ref[...] = dot(pick, arrived).astype(BF16)

    def image(i, carry):
        side, gain_sum = carry
        here = rows_of(i, tall)
        group = rows_of(i, slots)
        expert_sum, grad_slots = summed_ref[group, :features], summed_ref[group, features:]
        resid = resid_ref[here, :]
        cot = cot_ref[here, :]
        dispatch, combine = softmaxes(logit_ref[group, :], places, experts)
        output = resid + dot(combine.astype(BF16), expert_sum, TN)
        output_ref[i] = output[:places].astype(BF16)
        normed, factor = normalize(resid)
        act = (normed * gain).astype(BF16)
        grad_comb = dot(expert_sum, cot, NT)
        grad_disp = dot(grad_slots, act, NT)
        grad_logits = combine * (grad_comb - jnp.sum(grad_comb * combine, axis=0, keepdims=True))
        grad_logits = grad_logits + dispatch * (
            grad_disp - jnp.sum(grad_disp * dispatch, axis=1, keepdims=True)
        )
        grad_logits = grad_logits.astype(BF16)
        grad_act = dot(
            jnp.concatenate([dispatch.astype(BF16), grad_logits], axis=0),
            jnp.concatenate([grad_slots, router], axis=0),
            TN,
        )
        att = cot.astype(F32) + norm_back(grad_act * gain, normed, factor)
        att_ref[here, :] = att.astype(BF16)
        return (
            side + dot(grad_logits, act),
            gain_sum + jnp.sum(grad_act * normed, axis=0, keepdims=True),
        )

    side, gain_sum = lax.fori_loop(
        0, images, image, (jnp.zeros((slots, features), F32), jnp.zeros((1, features), F32))
    )

    @pl.loop(0, images // 2)
    def _(i):
        here = rows_of(i, 2 * tall)
        grad_mixed_ref[here, :] = dot(att_ref[here, :], weight[...], NT).astype(BF16)

    part = m0.shape[1]
    grad_w_ref[:part, :] = dot(m0[...], att_ref[...], TN).astype(BF16)
    grad_w_ref[part:, :] = dot(m1[...], att_ref[...], TN).astype(BF16)
    slot = iota((LANES, slots), 0) ^ order_ref[order_ref.shape[0] - 1]
    slot = jnp.where(iota((LANES, slots), 0) < experts, slot, -1)
    fits = jnp.where(slot == iota((LANES, slots), 1), 1.0, 0.0).astype(BF16)
    side = dot(fits, side.astype(BF16))
    side = jnp.where(iota(side.shape, 0) == experts, gain_sum, side)
    grad_side_ref[...] = side.T.astype(BF16)


def back(images, places, experts, order, resid, logits, cot, mixed, w, small, sources):
    total, features = resid.shape
    return call(
        functools.partial(back_body, images, places, experts),
        "back",
        (order, resid, logits, cot, *mixed, w, small, *sources),
        [
            ((images, places, features), BF16),
            ((total, features), BF16),
            ((total, features), BF16),
            ((features, features), BF16),
            ((features, LANES), BF16),
        ],
        [((logits.shape[0], 2 * features), BF16)],
        14,
        8 * total * features * features,
        hbm=(0,),
    )


def attend_back_body(images, extra, offset, order_ref, joint_ref, prob_ref, grad_ref, mixed_ref, act_ref, *refs):
    more, (out_ref, *targets, total) = refs[:extra], refs[extra:]
    width = joint_ref.shape[1]
    tall = joint_ref.shape[0] // images
    third = width // 3
    heads = prob_ref.shape[0] // images
    low = iota((tall, LANES), 1) < LANES // 2

    @pl.loop(0, images)
    def _(i):
        here = rows_of(i, tall)
        for pair in range(third // LANES):
            query, keys, values = (
                joint_ref[here, part * third + pair * LANES : part * third + (pair + 1) * LANES]
                for part in range(3)
            )
            grad = grad_ref[here, offset + pair * LANES : offset + (pair + 1) * LANES]
            product = grad.astype(F32) * mixed_ref[
                here, pair * LANES : (pair + 1) * LANES
            ].astype(F32)
            grads = []
            for side in range(2):
                mine = low if side == 0 else ~low
                prob = prob_ref[i * heads + 2 * pair + side]
                inner = jnp.sum(jnp.where(mine, product, 0.0), axis=1, keepdims=True)
                grad_prob = dot(jnp.where(mine, grad, 0), values, NT)
                grad_scores = (prob.astype(F32) * (grad_prob - inner) * 0.125).astype(BF16)
                grads.append(
                    (dot(grad_scores, keys), dot(grad_scores, query, TN), dot(prob, grad, TN))
                )
            for part in range(3):
                joined = jnp.where(low, grads[0][part], grads[1][part]).astype(BF16)
                out_ref[
                    here, part * third + pair * LANES : part * third + (pair + 1) * LANES
                ] = joined

    step = third
    for start in range(0, width, step):
        total[:, start : start + step] = dot(
            act_ref[...], out_ref[:, start : start + step], TN
        ).astype(BF16)
    store_blocks(order_ref, total, targets, slice(0, width))
    place = width
    for source in more:
        end = place + source.shape[1]
        store_blocks(order_ref, source, targets, slice(place, end))
        place = end


def attend_back(images, offset, order, joint, prob, grad_mixed, mixed, act, splits, more=()):
    total, width = joint.shape
    features = act.shape[1]
    columns = width + sum(m.shape[1] for m in more)
    parts = [((features // n, columns), BF16) for n in splits]
    return call(
        functools.partial(attend_back_body, images, len(more), offset),
        "attend_back",
        (order, joint, prob, grad_mixed, mixed, act, *more),
        [(joint.shape, BF16)] + parts,
        [((features, width), BF16)],
        16,
        2 * total * features * width * 4,
    )


def finish_body(images, places, token_ref, att_ref, j0, j1, s0, s1, small_ref, out_ref):
    total, features = token_ref.shape
    tall = total // images

    @pl.loop(0, images // 2)
    def _(i):
        here = rows_of(i, 2 * tall)
        grad_act = dot(j0[here, :], s0[...], NT) + dot(j1[here, :], s1[...], NT)
        normed, factor = normalize(token_ref[here, :].astype(F32))
        result = att_ref[here, :].astype(F32)
        result = result + norm_back(grad_act * small_ref[0:1, :], normed, factor)
        result = result.astype(BF16)
        out_ref[2 * i] = result[:places]
        out_ref[2 * i + 1] = result[tall : tall + places]


def finish(images, places, tokens, att, joints, weights, small):
    total, features = tokens.shape
    return call(
        functools.partial(finish_body, images, places),
        "finish",
        (tokens, att, *joints, *weights, small),
        [((images, places, features), BF16)],
        [],
        12,
        6 * total * features * features,
        hbm=(0,),
    )[0]


def per_device(
    tokens, cotangent, heads_in, heads_out, slot_router, first_gain, second_gain, expert_in, expert_out
):
    images, places, features = tokens.shape
    experts = slot_router.shape[1]
    group = lax.axis_size("grp")
    reps = lax.axis_size("rep")
    me = lax.axis_index("grp")
    own_rows = heads_in.shape[0]
    chip = me // 2
    odd = lax.axis_index("rep") % 2
    direct = group == 8
    ways = jnp.arange(8, dtype=jnp.int32)
    if direct:
        order = jnp.concatenate([ways ^ me, (ways % 4 * 2 + ways // 4) ^ me, odd[None], chip[None]])
    else:
        order = jnp.concatenate([ways, ways, odd[None], chip[None]])
    tall = -(-places // 16) * 16
    slot_rows = -(-experts // 16) * 16
    part = features // 3
    wide = 3 * part

    grow = ((0, 0), (0, tall - places), (0, 0))
    source = jnp.pad(tokens, grow).reshape(images * tall, features)
    cot = jnp.pad(cotangent, grow).reshape(images * tall, features)
    gains = jnp.stack([first_gain, second_gain])
    if direct:
        h0, h1, t0, t1 = prepare(heads_in, heads_out, slot_router, gains)
        head_first = gather_first((h0, h1))
        head_first = after(head_first, source, cot)
        (t0, t1), head_first = lax.optimization_barrier(((t0, t1), head_first))
        head_second = gather_second(join((h0, h1), head_first))
        tail_first = gather_first((t0, t1))
        head = gather_last((h0, h1), head_first, head_second)
        tail_first = after(tail_first, *head)
        tail_join = join((t0, t1), tail_first)
        source = after(source, *tail_join)
    else:
        thirds = [heads_in[:, k * features : (k + 1) * features] for k in range(3)]
        head_part = jnp.concatenate([t[:, :part] for t in thirds], axis=1)
        tail_part = jnp.concatenate([t[:, part:] for t in thirds] + [heads_out], axis=1)
        small = jnp.concatenate([gains, slot_router.T], axis=0)
        extra = -(-small.shape[0] // 16) * 16
        head_part = lax.all_gather(head_part, "grp", axis=0, tiled=True).reshape(8, -1, wide)
        small = lax.all_gather(small, "grp", axis=1, tiled=True).reshape(-1, 8, features // 8)
        small = small.transpose(1, 0, 2)
        small = jnp.pad(small, ((0, 0), (0, extra - small.shape[1]), (0, wide - small.shape[2])))
        head = as_gathered(jnp.concatenate([small, head_part], axis=1), extra + features // 16)
        tail_part = lax.all_gather(tail_part, "grp", axis=0, tiled=True)
        tail = as_gathered(tail_part.reshape(8, -1, 3 * features), features // 16)

    act, small, w_head, joint_head, prob_head, mixed_head = attend(
        True, images, places, order, source, head, wide
    )
    if direct:
        tail_second = after(gather_second(tail_join), mixed_head)
        tail = gather_last((t0, t1), tail_first, tail_second)
    w_out, w_tail, joint_tail, prob_tail, mixed_tail = attend(
        False, images, places, order, act, tail, 2 * wide
    )
    mixes = [mixed_head, mixed_tail]
    resid, logits, *leaving = route(
        images, places, experts, slot_rows, order, source, cot, mixes, w_out, small
    )

    arrived = [leaving[0]] + [swap(leaving[k], "grp", group, 2 * k) for k in range(1, experts)]
    arrived = arrived + [swap(part, "grp", group, 1) for part in arrived]
    piece_in, piece_out = expert_in[0], expert_out[0]
    received, kept, given = expert(images, piece_in, piece_out, arrived)
    both = pair_sum(kept, [swap(given, "grp", group, 1)], experts)
    summed = [both[0]] + [swap(both[k], "grp", group, 2 * k) for k in range(1, experts)]
    received = after(received, *summed)
    far = [swap(received, "rep", reps, k) for k in range(1, reps)]
    output, att, grad_mixed, grad_out, grad_side = back(
        images, places, experts, order, resid, logits, cot, mixes, w_out, small, summed
    )
    grad_mixed, far = lax.optimization_barrier((grad_mixed, far))
    grad_joint_tail, keep_tail, give_tail = attend_back(
        images, part, order, joint_tail, prob_tail, grad_mixed, mixed_tail, act, (2, 2), (grad_out, grad_side)
    )
    if direct:
        sums = pair_sum(keep_tail, [swap(give_tail, "grp", group, 1)], 4)
        others = [swap(sums[k], "grp", group, 2 * k) for k in range(1, 4)]
        grad_mixed = after(grad_mixed, *sums)
    grad_joint_head, keep_head, *give_head = attend_back(
        images, 0, order, joint_head, prob_head, grad_mixed, mixed_head, act, (2, 4, 4)
    )
    joints, weights = [grad_joint_head, grad_joint_tail], [w_head, w_tail]
    every = [received] + far
    if direct:
        got = [swap(part, "grp", group, 1) for part in give_head]
        own, others = after((sums[0], others), got)
        mine, give = split_sum(order, own, *others)
        other = swap(give, "rep", reps, 1)
        sums = pair_sum(keep_head, got, 4)
        others = [swap(sums[k], "grp", group, 2 * k) for k in range(1, 4)]
        att = after(att, mine, *sums)
        token_grad = finish(images, places, source, att, joints, weights, small)
        own, others, other = after((sums[0], others, other), token_grad)
        tail_sum = total_sum(mine, other)
        head_sum = total_sum(own, *others)
        every, tail_sum, head_sum = after((every, tail_sum, head_sum), token_grad)
        tail_other = swap(tail_sum, "rep", reps, 2)
        head_other = swap(head_sum, "rep", reps, 1)
        expert_in_grad, expert_out_grad = expert_grad(every, piece_in, piece_out)
        tail_other, head_other = after((tail_other, head_other), expert_in_grad)
        tail_sum, head_sum = total_sum(tail_sum, tail_other), total_sum(head_sum, head_other)
        tail_other = swap(tail_sum, "rep", reps, 1)
        head_other = swap(head_sum, "rep", reps, 3)
        heads_in_grad, heads_out_grad, router_grad, gain_one_grad, gain_two_grad = shares(
            experts, order, head_sum, head_other, tail_sum, tail_other, heads_in, first_gain[None]
        )
        gain_one_grad, gain_two_grad = gain_one_grad[0], gain_two_grad[0]
    else:
        token_grad = finish(images, places, source, att, joints, weights, small)
        expert_in_grad, expert_out_grad = expert_grad(every, piece_in, piece_out)
        tail_sum = jnp.concatenate([keep_tail, give_tail])
        tail_sum = lax.psum_scatter(tail_sum, "grp", scatter_dimension=0, tiled=True)
        head_sum = jnp.concatenate([keep_head, *give_head])
        head_sum = lax.psum_scatter(head_sum, "grp", scatter_dimension=0, tiled=True)
        tail_sum = lax.psum(tail_sum, "rep").astype(F32)
        head_sum = lax.psum(head_sum, "rep").astype(F32)
        columns = []
        for k in range(3):
            columns.append(head_sum[:, k * part : (k + 1) * part])
            columns.append(tail_sum[:, 2 * k * part : 2 * (k + 1) * part])
        heads_in_grad = jnp.concatenate(columns, axis=1)
        gain_one_grad = jnp.sum(heads_in_grad * heads_in.astype(F32), axis=1)
        gain_one_grad = gain_one_grad / first_gain.astype(F32)
        heads_out_grad, rest = tail_sum[:, 2 * wide : 3 * wide], tail_sum[:, 3 * wide :]
        router_grad, gain_two_grad = rest[:, :experts], rest[:, experts]
    return (
        output,
        token_grad,
        heads_in_grad,
        heads_out_grad,
        router_grad,
        gain_one_grad,
        gain_two_grad,
        expert_in_grad[None],
        expert_out_grad[None],
    )


def solution(mesh):
    token_spec = P(("rep", "grp"), None, None)
    matrix, vector, stack = P("grp", None), P("grp"), P("grp", None, None)
    return jax.shard_map(
        per_device,
        mesh=mesh,
        in_specs=(token_spec, token_spec, matrix, matrix, matrix, vector, vector, stack, stack),
        out_specs=(token_spec, token_spec, matrix, matrix, matrix, vector, vector, stack, stack),
        check_vma=False,
    )
```

time: 751 us -> 188 us (0.25)
  waiting for transfers between devices: 445 us -> 36.5 us
  matrix products: 137 us -> 0 us
  Pallas kernels: 0 us -> 96.3 us
  blocking collectives: 48.7 us -> 0 us
  other arithmetic: 40.3 us -> 0.77 us
  local copies, waits for them, and re-layouts: 43.4 us -> 13.4 us
  starting transfers between devices: 14.3 us -> 39.2 us
  between operations: 16.3 us -> 0.93 us
    psum x1 -> x0, waiting for transfers between devices: 355 us -> none  [per_device(): lax.psum((rowed[0], rowed[1], rowed[2], rowed[3], rowed[4], expert_in_ter...]
    dot_general x27 -> x0, matrix products: 137 us -> none  [the longest x25 134 us: mult(): return jnp.einsum(form, left, right, preferred_element_type=jnp.float32)]
    pallas_call x0 -> x21, Pallas kernels: none -> 96.3 us  [the longest x20 89.6 us: call(): pl.pallas_call(body, in_specs=[SM if x.dtype == jnp.int32 else VM for x i...]
    reduce_scatter x2 -> x0, waiting for transfers between devices: 69.5 us -> none  [the longest x1 69.3 us: per_device(): lax.psum_scatter(grad_heads_in, 'grp', scatter_dimension=0, tiled=True)]
    ppermute x0 -> x48, starting transfers between devices: none -> 39.2 us  [swap(): lax.ppermute(values, axis, [(place, place ^ bit) for place in range(size)])]
    ppermute x0 -> x48, waiting for transfers between devices: none -> 36.5 us  [swap(): lax.ppermute(values, axis, [(place, place ^ bit) for place in range(size)])]
    unnamed x2 -> x0, blocking collectives: 28.4 us -> none
    convert_element_type x5 -> x0, other arithmetic: 16 us -> none  [the longest x1 10.7 us: per_device(): grad_scores = grad_scores.astype(jnp.bfloat16)]
  transfers between devices with their start and end apart: 10 -> 48, of which waited for: 9 -> 24; matrix products, arithmetic and copies ran while one was open for 17% -> 2% of each run, Pallas kernels for 0% -> 27%
where the time goes in v1:
time: 188 us; the launch traced here: 187 us
  Pallas kernels  96.3 us (51%)
  starting transfers between devices  39.2 us (21%)
  waiting for transfers between devices  36.5 us (19%)
  local copies, waits for them, and re-layouts  13.4 us (7%)
    pallas_call x20, Pallas kernels, call(): pl.pallas_call(body, in_specs=[SM if x.dtype == jnp.int32 else VM for x i...  89.6 us
    ppermute x48, starting transfers between devices, swap(): lax.ppermute(values, axis, [(place, place ^ bit) for place in range(size)])  39.2 us
    ppermute x48, waiting for transfers between devices, swap(): lax.ppermute(values, axis, [(place, place ^ bit) for place in range(size)])  36.5 us
    unnamed x34, local copies, waits for them, and re-layouts  10.4 us
    pallas_call x1, Pallas kernels, expert_grad(): pl.pallas_call(functools.partial(expert_grad_body, len(sources)), grid=(h...  6.66 us
  transfers between devices with their start and end apart: 48, of which 24 were waited for; matrix products, arithmetic and copies ran while one was open for 2% of the time, Pallas kernels for 27%

profile of v1, /device:TPU:0, one launch (start us, length us, event | category | flops | bytes accessed | tf_op | source)
XLA Modules:
  0.0 187.1 jit_solution(17691744343622384679)
XLA Ops:
  4.1 3.0 %collective-permute-start = (bf16[64,768]{1,0:T(8,128)(2,1)S(1)}, bf16[64,768]{1,0:T(8,128)(2,1)S(1)}, u32[]{:S(2)}, u32[]{:S(2)}) collective-permute-start(bf16[64,768]{1,0:T(8,128)(2,1)S(1)} %get-tuple-element.107.a0.refs_0_), channel_id=1, source_target_pairs={{0,2},{1,3},{2,0},{3,1},{4,6},{5,7},{6,4},{7,5},{8,10},{9,11},{10,... | collective-permute-start | bytes 294920 | tf_op jit(solution)/shard_map/ppermute | solution.py:26
  8.6 1.6 pad.7
  22.1 2.0 %collective-permute-done.2.a1.refs_2_ = bf16[48,2304]{1,0:T(8,128)(2,1)S(1)} collective-permute-done((bf16[48,2304]{1,0:T(8,128)(2,1)S(1)}, bf16[48,2304]{1,0:T(8,128)(2,1)S(1)}, u32[]{:S(2)}, u32[]{:S(2)}) %collective-permute-start.2) | collective-permute-done | bytes 221216 | tf_op jit(solution)/shard_map/ppermute | solution.py:26
  29.1 11.3 %attend.2 = (bf16[1248,768]{1,0:T(8,128)(2,1)S(1)}, f32[16,768]{1,0:T(8,128)S(1)}, bf16[768,768]{1,0:T(8,128)(2,1)S(1)}, bf16[1248,768]{1,0:T(8,128)(2,1)S(1)}, ...) custom-call(s32[18]{0:T(128)S(1)} %pad_add_fusion.order_ref, bf16[1248,768]{1,0:T(8,128)(2,1)S(1)} %bitcast.16, ...), custom_call_target="tpu_custom_call" | custom-call | flops 2944401408 | bytes 1000000 | tf_op jit(solution)/shard_map/attend/pallas_call | solution.py:128
  44.0 13.3 %attend.3 = (bf16[768,768]{1,0:T(8,128)(2,1)S(1)}, bf16[768,1536]{1,0:T(8,128)(2,1)S(1)}, bf16[1248,1536]{1,0:T(8,128)(2,1)S(1)}, bf16[48,208,208]{2,1,0:T(8,128)(2,1)S(1)}, bf16[1248,512]{1,0:T(8,128)(2,1)S(1)}) custom-call(s32[18]{0:T(128)S(1)} %pad_add_fusion.order_ref, bf16[1248,768]{1,0:T(8,128)(2,1)S(1)} %get-tuple-element.123.source_ref.act_ref, ...), custom_call_target="tpu_custom_call" | custom-call | flops 5888802816 | bytes 1000000 | tf_op jit(solution)/shard_map/attend/pallas_call | solution.py:128
  57.4 8.4 %route.1 = (f32[1248,768]{1,0:T(8,128)S(1)}, f32[96,208]{1,0:T(8,128)S(1)}, bf16[8,1536]{1,0:T(8,128)(2,1)S(1)}, bf16[8,1536]{1,0:T(8,128)(2,1)S(1)}, bf16[8,153...) custom-call(s32[18]{0:T(128)S(1)} %pad_add_fusion.order_ref, bf16[1248,768]{1,0:T(8,128)(2,1)S(1)} %bitcast.17, ...), custom_call_target="tpu_custom_call" | custom-call | flops 2944401408 | bytes 1000000 | tf_op jit(solution)/shard_map/route/pallas_call | solution.py:128
  71.2 2.2 %collective-permute-done.22.refs_3_ = bf16[8,1536]{1,0:T(8,128)(2,1)S(1)} collective-permute-done((bf16[8,1536]{1,0:T(8,128)(2,1)S(1)}, bf16[8,1536]{1,0:T(8,128)(2,1)S(1)}, u32[]{:S(2)}, u32[]{:S(2)}) %collective-permute-start.22) | collective-permute-done | bytes 24608 | tf_op jit(solution)/shard_map/ppermute | solution.py:26
  74.6 2.4 %expert.1 = (bf16[48,1536]{1,0:T(8,128)(2,1)S(1)}, bf16[32,1536]{1,0:T(8,128)(2,1)S(1)}, bf16[32,1536]{1,0:T(8,128)(2,1)S(1)}) custom-call(bf16[768,1536]{1,0:T(8,128)(2,1)S(1)} %bitcast.12, bf16[1536,768]{1,0:T(8,128)(2,1)S(1)} %bitcast.14, bf16[8,1536]{1,0:T(8,128)(2,1)S(1)} %get-tuple-element.131.refs_0_, ...), custom_call_target="tpu_custom_call" | custom-call | flops 1000000000 | bytes 1000000 | tf_op jit(solution)/shard_map/expert/pallas_call | solution.py:128
  79.7 2.3 %collective-permute-start.30 = (bf16[8,1536]{1,0:T(8,128)(2,1)S(1)}, bf16[8,1536]{1,0:T(8,128)(2,1)S(1)}, u32[]{:S(2)}, u32[]{:S(2)}) collective-permute-start(bf16[8,1536]{1,0:T(8,128)(2,1)S(1)} %get-tuple-element.140), channel_id=1, source_target_pairs={{0,6},{1,7},{2,4},{3,5},{4,2},{5,3},{6,0},{7,1},{8,14},{9,15},{10,... | collective-permute-start | bytes 73736 | tf_op jit(solution)/shard_map/ppermute | solution.py:26
  82.9 1.6 collective-permute-done.30.refs_3_
  84.5 3.6 %collective-permute-start.33 = (bf16[48,1536]{1,0:T(8,128)(2,1)S(1)}, bf16[48,1536]{1,0:T(8,128)(2,1)S(1)}, u32[]{:S(2)}, u32[]{:S(2)}) collective-permute-start(bf16[48,1536]{1,0:T(8,128)(2,1)S(1)} %get-tuple-element.188.refs_0_), channel_id=1, source_target_pairs={{0,24},{8,16},{16,8},{24,0},{1,25},{9,17},{17,9},{25,1},{2,26},{10... | collective-permute-start | bytes 442376 | tf_op jit(solution)/shard_map/ppermute | solution.py:26
  88.8 12.5 %back.1 = (bf16[6,197,768]{2,1,0:T(8,128)(2,1)}, bf16[1248,768]{1,0:T(8,128)(2,1)S(1)}, bf16[1248,768]{1,0:T(8,128)(2,1)S(1)}, bf16[768,768]{1,0:T(8,128)(2,1)S(1)}, bf16[768,128]{1,0:T(8,128)(2,1)S(1)}) custom-call(s32[18]{0:T(128)S(1)} %pad_add_fusion.order_ref, f32[1248,768]{1,0:T(8,128)S(1)} %get-tuple-element.129.resid_ref, ...), custom_call_target="tpu_custom_call" | custom-call | flops 5888802816 | bytes 1000000 | tf_op jit(solution)/shard_map/back/pallas_call | solution.py:128
  101.4 2.4 %copy-done.14 = bf16[48,208,208]{2,1,0:T(8,128)(2,1)S(1)} copy-done((bf16[48,208,208]{2,1,0:T(8,128)(2,1)S(1)}, bf16[48,208,208]{2,1,0:T(8,128)(2,1)}, u32[]{:S(2)}) %copy-start.14) | copy-done | bytes 4153368
  103.8 18.9 %attend_back.2 = (bf16[1248,1536]{1,0:T(8,128)(2,1)S(1)}, bf16[384,2432]{1,0:T(8,128)(2,1)S(1)}, bf16[384,2432]{1,0:T(8,128)(2,1)S(1)}) custom-call(s32[18]{0:T(128)S(1)} %pad_add_fusion.order_ref, bf16[1248,1536]{1,0:T(8,128)(2,1)S(1)} %get-tuple-element.143.joint_ref, bf16[48,208,208]{2,1,0:T(8,128)(2,1)S(1)} %copy-done.14, ...), custom_call_target="tpu_custom_call" | custom-call | flops 11777605632 | bytes 1000000 | tf_op jit(solution)/shard_map/attend_back/pallas_call | solution.py:128
  122.8 3.8 %collective-permute-done.34.refs_0_ = bf16[384,2432]{1,0:T(8,128)(2,1)S(1)} collective-permute-done((bf16[384,2432]{1,0:T(8,128)(2,1)S(1)}, bf16[384,2432]{1,0:T(8,128)(2,1)S(1)}, u32[]{:S(2)}, u32[]{:S(2)}) %collective-permute-start.34) | collective-permute-done | bytes 1867808 | tf_op jit(solution)/shard_map/ppermute | solution.py:26
  130.6 10.3 %attend_back.3 = (bf16[1248,768]{1,0:T(8,128)(2,1)S(1)}, bf16[384,768]{1,0:T(8,128)(2,1)S(1)}, bf16[192,768]{1,0:T(8,128)(2,1)S(1)}, bf16[192,768]{1,0:T(8,128)(2,1)S(1)}) custom-call(s32[18]{0:T(128)S(1)} %pad_add_fusion.order_ref, bf16[1248,768]{1,0:T(8,128)(2,1)S(1)} %get-tuple-element.157.joint_ref, ...), custom_call_target="tpu_custom_call" | custom-call | flops 5888802816 | bytes 1000000 | tf_op jit(solution)/shard_map/attend_back/pallas_call | solution.py:128
  146.7 4.5 %collective-permute-done.36.refs_2_ = bf16[96,2432]{1,0:T(8,128)(2,1)S(1)} collective-permute-done((bf16[96,2432]{1,0:T(8,128)(2,1)S(1)}, bf16[96,2432]{1,0:T(8,128)(2,1)S(1)}, u32[]{:S(2)}, u32[]{:S(2)}) %collective-permute-start.36) | collective-permute-done | bytes 466976 | tf_op jit(solution)/shard_map/ppermute | solution.py:26
  153.7 7.8 %finish.1 = bf16[6,197,768]{2,1,0:T(8,128)(2,1)} custom-call(bf16[1248,768]{1,0:T(8,128)(2,1)S(1)} %bitcast.18, bf16[1248,768]{1,0:T(8,128)(2,1)S(1)} %get-tuple-element.172.att_ref, bf16[1248,768]{1,0:T(8,128)(2,1)S(1)} %get-tuple-element.173.j0, bf16[1248,1536]{1,0:T(8,128)(2,1)S(1)} %get-tuple-element.174.j1, bf16[768,768]{1,0:T(8,128)(2,1)S(1)} %get-tuple-element.175.s0, ...), custom_call_target="tpu_custom_call" | custom-call | flops 4416602112 | bytes 1000000 | tf_op jit(solution)/shard_map/finish/pallas_call | solution.py:128
  161.7 3.0 %collective-permute-start.44 = (bf16[48,2432]{1,0:T(8,128)(2,1)S(1)}, bf16[48,2432]{1,0:T(8,128)(2,1)S(1)}, u32[]{:S(2)}, u32[]{:S(2)}) collective-permute-start(bf16[48,2432]{1,0:T(8,128)(2,1)S(1)} %total_sum.4.refs_0_), channel_id=1, source_target_pairs={{0,16},{8,24},{16,0},{24,8},{1,17},{9,25},{17,1},{25,9},{2,18},{10... | collective-permute-start | bytes 700424 | tf_op jit(solution)/shard_map/ppermute | solution.py:26
  164.7 6.7 %expert_grad.1 = (f32[768,1536]{1,0:T(8,128)}, f32[1536,768]{1,0:T(8,128)}) custom-call(bf16[48,1536]{1,0:T(8,128)(2,1)S(1)} %get-tuple-element.188.refs_0_, bf16[48,1536]{1,0:T(8,128)(2,1)S(1)} %collective-permute-done.31.refs_1_, bf16[48,1536]{1,0:T(8,128)(2,1)S(1)} %collective-permute-done.32.refs_2_, ...), custom_call_target="tpu_custom_call" | custom-call | flops 1887436800 | bytes 14000000 | tf_op jit(solution)/shard_map/expert_grad/pallas_call | solution.py:515
  171.4 2.4 %collective-permute-done.44.refs_1_ = bf16[48,2432]{1,0:T(8,128)(2,1)S(1)} collective-permute-done((bf16[48,2432]{1,0:T(8,128)(2,1)S(1)}, bf16[48,2432]{1,0:T(8,128)(2,1)S(1)}, u32[]{:S(2)}, u32[]{:S(2)}) %collective-permute-start.44) | collective-permute-done | bytes 233504 | tf_op jit(solution)/shard_map/ppermute | solution.py:26
  174.0 2.5 %collective-permute-start.46 = (bf16[96,768]{1,0:T(8,128)(2,1)S(1)}, bf16[96,768]{1,0:T(8,128)(2,1)S(1)}, u32[]{:S(2)}, u32[]{:S(2)}) collective-permute-start(bf16[96,768]{1,0:T(8,128)(2,1)S(1)} %total_sum.6.head_ref), channel_id=1, source_target_pairs={{0,24},{8,16},{16,8},{24,0},{1,25},{9,17},{17,9},{25,1},{2,26},{10... | collective-permute-start | bytes 442376 | tf_op jit(solution)/shard_map/ppermute | solution.py:26
  176.5 7.8 %collective-permute-done.46.head_other = bf16[96,768]{1,0:T(8,128)(2,1)S(1)} collective-permute-done((bf16[96,768]{1,0:T(8,128)(2,1)S(1)}, bf16[96,768]{1,0:T(8,128)(2,1)S(1)}, u32[]{:S(2)}, u32[]{:S(2)}) %collective-permute-start.46) | collective-permute-done | bytes 147488 | tf_op jit(solution)/shard_map/ppermute | solution.py:26
  184.7 1.7 shares.1
  (132 shorter events, 50.0 us)
Async XLA Ops:
  4.1 7.5 %collective-permute-start = (bf16[64,768]{1,0:T(8,128)(2,1)S(1)}, bf16[64,768]{1,0:T(8,128)(2,1)S(1)}, u32[]{:S(2)}, u32[]{:S(2)}) collective-permute-start(bf16[64,768]{1,0:T(8,128)(2,1)S(1)} %get-tuple-element.107.a0.refs_0_), channel_id=1, source_target_pairs={{0,2},{1,3},{2,0},{3,1},{4,6},{5,7},{6,4},{7,5},{8,10},{9,11},{10,... | collective-permute-start | bytes 294920 | tf_op jit(solution)/shard_map/ppermute | solution.py:26
  11.7 6.1 %collective-permute-start.4 = (bf16[128,768]{1,0:T(8,128)(2,1)S(1)}, bf16[128,768]{1,0:T(8,128)(2,1)S(1)}, u32[]{:S(2)}, u32[]{:S(2)}) collective-permute-start(bf16[128,768]{1,0:T(8,128)(2,1)S(1)} %get-tuple-element.115), channel_id=1, source_target_pairs={{0,4},{1,5},{2,6},{3,7},{4,0},{5,1},{6,2},{7,3},{8,12},{9,13},{10,... | collective-permute-start | bytes 589832 | tf_op jit(solution)/shard_map/ppermute | solution.py:26
  13.1 6.8 %collective-permute-start.5 = (bf16[96,768]{1,0:T(8,128)(2,1)S(1)}, bf16[96,768]{1,0:T(8,128)(2,1)}, u32[]{:S(2)}, u32[]{:S(2)}) collective-permute-start(bf16[96,768]{1,0:T(8,128)(2,1)S(1)} %get-tuple-element.116), channel_id=1, source_target_pairs={{0,2},{1,3},{2,0},{3,1},{4,6},{5,7},{6,4},{7,5},{8,10},{9,11},{10,... | collective-permute-start | bytes 442376 | tf_op jit(solution)/shard_map/ppermute | solution.py:26
  13.8 10.2 %collective-permute-start.2 = (bf16[48,2304]{1,0:T(8,128)(2,1)S(1)}, bf16[48,2304]{1,0:T(8,128)(2,1)S(1)}, u32[]{:S(2)}, u32[]{:S(2)}) collective-permute-start(bf16[48,2304]{1,0:T(8,128)(2,1)S(1)} %get-tuple-element.111.a0.refs_0_), channel_id=1, source_target_pairs={{0,2},{1,3},{2,0},{3,1},{4,6},{5,7},{6,4},{7,5},{8,10},{9,11},{10,... | collective-permute-start | bytes 663560 | tf_op jit(solution)/shard_map/ppermute | solution.py:26
  16.0 8.1 %collective-permute-start.3 = (bf16[48,2304]{1,0:T(8,128)(2,1)S(1)}, bf16[48,2304]{1,0:T(8,128)(2,1)S(1)}, u32[]{:S(2)}, u32[]{:S(2)}) collective-permute-start(bf16[48,2304]{1,0:T(8,128)(2,1)S(1)} %get-tuple-element.112.b0.refs_1_), channel_id=1, source_target_pairs={{0,4},{1,5},{2,6},{3,7},{4,0},{5,1},{6,2},{7,3},{8,12},{9,13},{10,... | collective-permute-start | bytes 663560 | tf_op jit(solution)/shard_map/ppermute | solution.py:26
  17.8 6.3 %collective-permute-start.10 = (bf16[128,768]{1,0:T(8,128)(2,1)S(1)}, bf16[128,768]{1,0:T(8,128)(2,1)S(1)}, u32[]{:S(2)}, u32[]{:S(2)}) collective-permute-start(bf16[128,768]{1,0:T(8,128)(2,1)S(1)} %collective-permute-done.4.refs_4_), channel_id=1, source_target_pairs={{0,1},{1,0},{2,3},{3,2},{4,5},{5,4},{6,7},{7,6},{8,9},{9,8},{10,11... | collective-permute-start | bytes 589832 | tf_op jit(solution)/shard_map/ppermute | solution.py:26
  25.1 15.4 %collective-permute-start.12 = (bf16[96,2304]{1,0:T(8,128)(2,1)}, bf16[96,2304]{1,0:T(8,128)(2,1)}, u32[]{:S(2)}, u32[]{:S(2)}) collective-permute-start(bf16[96,2304]{1,0:T(8,128)(2,1)} %get-tuple-element.119), channel_id=1, source_target_pairs={{0,4},{1,5},{2,6},{3,7},{4,0},{5,1},{6,2},{7,3},{8,12},{9,13},{10,... | collective-permute-start | bytes 1327112 | tf_op jit(solution)/shard_map/ppermute | solution.py:26
  25.8 14.7 %collective-permute-start.13 = (bf16[96,2304]{1,0:T(8,128)(2,1)}, bf16[96,2304]{1,0:T(8,128)(2,1)}, u32[]{:S(2)}, u32[]{:S(2)}) collective-permute-start(bf16[96,2304]{1,0:T(8,128)(2,1)} %get-tuple-element.120), channel_id=1, source_target_pairs={{0,2},{1,3},{2,0},{3,1},{4,6},{5,7},{6,4},{7,5},{8,10},{9,11},{10,... | collective-permute-start | bytes 1327112 | tf_op jit(solution)/shard_map/ppermute | solution.py:26
  26.4 15.2 %collective-permute-start.14 = (bf16[48,2304]{1,0:T(8,128)(2,1)S(1)}, bf16[48,2304]{1,0:T(8,128)(2,1)S(1)}, u32[]{:S(2)}, u32[]{:S(2)}) collective-permute-start(bf16[48,2304]{1,0:T(8,128)(2,1)S(1)} %get-tuple-element.111.a0.refs_0_), channel_id=1, source_target_pairs={{0,1},{1,0},{2,3},{3,2},{4,5},{5,4},{6,7},{7,6},{8,9},{9,8},{10,11... | collective-permute-start | bytes 663560 | tf_op jit(solution)/shard_map/ppermute | solution.py:26
  68.7 4.7 %collective-permute-start.22 = (bf16[8,1536]{1,0:T(8,128)(2,1)S(1)}, bf16[8,1536]{1,0:T(8,128)(2,1)S(1)}, u32[]{:S(2)}, u32[]{:S(2)}) collective-permute-start(bf16[8,1536]{1,0:T(8,128)(2,1)S(1)} %get-tuple-element.134), channel_id=1, source_target_pairs={{0,6},{1,7},{2,4},{3,5},{4,2},{5,3},{6,0},{7,1},{8,14},{9,15},{10,... | collective-permute-start | bytes 73736 | tf_op jit(solution)/shard_map/ppermute | solution.py:26
  84.5 16.9 %collective-permute-start.33 = (bf16[48,1536]{1,0:T(8,128)(2,1)S(1)}, bf16[48,1536]{1,0:T(8,128)(2,1)S(1)}, u32[]{:S(2)}, u32[]{:S(2)}) collective-permute-start(bf16[48,1536]{1,0:T(8,128)(2,1)S(1)} %get-tuple-element.188.refs_0_), channel_id=1, source_target_pairs={{0,24},{8,16},{16,8},{24,0},{1,25},{9,17},{17,9},{25,1},{2,26},{10... | collective-permute-start | bytes 442376 | tf_op jit(solution)/shard_map/ppermute | solution.py:26
  88.1 13.3 %collective-permute-start.32 = (bf16[48,1536]{1,0:T(8,128)(2,1)S(1)}, bf16[48,1536]{1,0:T(8,128)(2,1)S(1)}, u32[]{:S(2)}, u32[]{:S(2)}) collective-permute-start(bf16[48,1536]{1,0:T(8,128)(2,1)S(1)} %get-tuple-element.188.refs_0_), channel_id=1, source_target_pairs={{0,16},{8,24},{16,0},{24,8},{1,17},{9,25},{17,1},{25,9},{2,18},{10... | collective-permute-start | bytes 442376 | tf_op jit(solution)/shard_map/ppermute | solution.py:26
  88.1 13.3 %collective-permute-start.31 = (bf16[48,1536]{1,0:T(8,128)(2,1)S(1)}, bf16[48,1536]{1,0:T(8,128)(2,1)S(1)}, u32[]{:S(2)}, u32[]{:S(2)}) collective-permute-start(bf16[48,1536]{1,0:T(8,128)(2,1)S(1)} %get-tuple-element.188.refs_0_), channel_id=1, source_target_pairs={{0,8},{8,0},{16,24},{24,16},{1,9},{9,1},{17,25},{25,17},{2,10},{10... | collective-permute-start | bytes 442376 | tf_op jit(solution)/shard_map/ppermute | solution.py:26
  127.0 18.9 %collective-permute-start.35 = (bf16[96,2432]{1,0:T(8,128)(2,1)S(1)}, bf16[96,2432]{1,0:T(8,128)(2,1)S(1)}, u32[]{:S(2)}, u32[]{:S(2)}) collective-permute-start(bf16[96,2432]{1,0:T(8,128)(2,1)S(1)} %get-tuple-element.154), channel_id=1, source_target_pairs={{0,2},{1,3},{2,0},{3,1},{4,6},{5,7},{6,4},{7,5},{8,10},{9,11},{10,... | collective-permute-start | bytes 1400840 | tf_op jit(solution)/shard_map/ppermute | solution.py:26
  128.6 22.6 %collective-permute-start.36 = (bf16[96,2432]{1,0:T(8,128)(2,1)S(1)}, bf16[96,2432]{1,0:T(8,128)(2,1)S(1)}, u32[]{:S(2)}, u32[]{:S(2)}) collective-permute-start(bf16[96,2432]{1,0:T(8,128)(2,1)S(1)} %get-tuple-element.155), channel_id=1, source_target_pairs={{0,4},{1,5},{2,6},{3,7},{4,0},{5,1},{6,2},{7,3},{8,12},{9,13},{10,... | collective-permute-start | bytes 1400840 | tf_op jit(solution)/shard_map/ppermute | solution.py:26
  129.9 21.5 %collective-permute-start.37 = (bf16[96,2432]{1,0:T(8,128)(2,1)S(1)}, bf16[96,2432]{1,0:T(8,128)(2,1)S(1)}, u32[]{:S(2)}, u32[]{:S(2)}) collective-permute-start(bf16[96,2432]{1,0:T(8,128)(2,1)S(1)} %get-tuple-element.156), channel_id=1, source_target_pairs={{0,6},{1,7},{2,4},{3,5},{4,2},{5,3},{6,0},{7,1},{8,14},{9,15},{10,... | collective-permute-start | bytes 1400840 | tf_op jit(solution)/shard_map/ppermute | solution.py:26
  143.1 18.4 %collective-permute-start.40 = (bf16[96,768]{1,0:T(8,128)(2,1)S(1)}, bf16[96,768]{1,0:T(8,128)(2,1)S(1)}, u32[]{:S(2)}, u32[]{:S(2)}) collective-permute-start(bf16[96,768]{1,0:T(8,128)(2,1)S(1)} %get-tuple-element.169), channel_id=1, source_target_pairs={{0,2},{1,3},{2,0},{3,1},{4,6},{5,7},{6,4},{7,5},{8,10},{9,11},{10,... | collective-permute-start | bytes 442376 | tf_op jit(solution)/shard_map/ppermute | solution.py:26
  144.7 16.9 %collective-permute-start.41 = (bf16[96,768]{1,0:T(8,128)(2,1)S(1)}, bf16[96,768]{1,0:T(8,128)(2,1)S(1)}, u32[]{:S(2)}, u32[]{:S(2)}) collective-permute-start(bf16[96,768]{1,0:T(8,128)(2,1)S(1)} %get-tuple-element.170), channel_id=1, source_target_pairs={{0,4},{1,5},{2,6},{3,7},{4,0},{5,1},{6,2},{7,3},{8,12},{9,13},{10,... | collective-permute-start | bytes 442376 | tf_op jit(solution)/shard_map/ppermute | solution.py:26
  146.0 15.6 %collective-permute-start.42 = (bf16[96,768]{1,0:T(8,128)(2,1)S(1)}, bf16[96,768]{1,0:T(8,128)(2,1)S(1)}, u32[]{:S(2)}, u32[]{:S(2)}) collective-permute-start(bf16[96,768]{1,0:T(8,128)(2,1)S(1)} %get-tuple-element.171), channel_id=1, source_target_pairs={{0,6},{1,7},{2,4},{3,5},{4,2},{5,3},{6,0},{7,1},{8,14},{9,15},{10,... | collective-permute-start | bytes 442376 | tf_op jit(solution)/shard_map/ppermute | solution.py:26
  152.4 9.1 %collective-permute-start.43 = (bf16[48,2432]{1,0:T(8,128)(2,1)S(1)}, bf16[48,2432]{1,0:T(8,128)(2,1)S(1)}, u32[]{:S(2)}, u32[]{:S(2)}) collective-permute-start(bf16[48,2432]{1,0:T(8,128)(2,1)S(1)} %get-tuple-element.180), channel_id=1, source_target_pairs={{0,8},{8,0},{16,24},{24,16},{1,9},{9,1},{17,25},{25,17},{2,10},{10... | collective-permute-start | bytes 700424 | tf_op jit(solution)/shard_map/ppermute | solution.py:26
  161.7 12.0 %collective-permute-start.44 = (bf16[48,2432]{1,0:T(8,128)(2,1)S(1)}, bf16[48,2432]{1,0:T(8,128)(2,1)S(1)}, u32[]{:S(2)}, u32[]{:S(2)}) collective-permute-start(bf16[48,2432]{1,0:T(8,128)(2,1)S(1)} %total_sum.4.refs_0_), channel_id=1, source_target_pairs={{0,16},{8,24},{16,0},{24,8},{1,17},{9,25},{17,1},{25,9},{2,18},{10... | collective-permute-start | bytes 700424 | tf_op jit(solution)/shard_map/ppermute | solution.py:26
  164.7 6.7 %collective-permute-start.45 = (bf16[96,768]{1,0:T(8,128)(2,1)S(1)}, bf16[96,768]{1,0:T(8,128)(2,1)S(1)}, u32[]{:S(2)}, u32[]{:S(2)}) collective-permute-start(bf16[96,768]{1,0:T(8,128)(2,1)S(1)} %total_sum.5.refs_0_), channel_id=1, source_target_pairs={{0,8},{8,0},{16,24},{24,16},{1,9},{9,1},{17,25},{25,17},{2,10},{10... | collective-permute-start | bytes 442376 | tf_op jit(solution)/shard_map/ppermute | solution.py:26
  173.8 10.8 %collective-permute-start.47 = (bf16[48,2432]{1,0:T(8,128)(2,1)S(1)}, bf16[48,2432]{1,0:T(8,128)(2,1)S(1)}, u32[]{:S(2)}, u32[]{:S(2)}) collective-permute-start(bf16[48,2432]{1,0:T(8,128)(2,1)S(1)} %total_sum.7.tail_ref), channel_id=1, source_target_pairs={{0,8},{8,0},{16,24},{24,16},{1,9},{9,1},{17,25},{25,17},{2,10},{10... | collective-permute-start | bytes 700424 | tf_op jit(solution)/shard_map/ppermute | solution.py:26
  174.0 10.4 %collective-permute-start.46 = (bf16[96,768]{1,0:T(8,128)(2,1)S(1)}, bf16[96,768]{1,0:T(8,128)(2,1)S(1)}, u32[]{:S(2)}, u32[]{:S(2)}) collective-permute-start(bf16[96,768]{1,0:T(8,128)(2,1)S(1)} %total_sum.6.head_ref), channel_id=1, source_target_pairs={{0,24},{8,16},{16,8},{24,0},{1,25},{9,17},{17,9},{25,1},{2,26},{10... | collective-permute-start | bytes 442376 | tf_op jit(solution)/shard_map/ppermute | solution.py:26
  (40 other events, 188.8 us)
